TPU v7x, 32 devices: a whole 2x2x4 slice. The times are simulated.
32 devices in a mesh: seq: 8 (over z, y), head: 4 (over x, core).
Axes of the slice: x: 2, y: 2, z: 4, core: 2. Of those that a mesh axis runs over, the one named last changes fastest.
Arguments:
- queries: bfloat16 [4096, 8192], P(('seq', 'head')), may hold values from -18 to 18
- keys: bfloat16 [4096, 1024], P(('seq', 'head')), may hold values from -6 to 6
- values: bfloat16 [4096, 1024], P(('seq', 'head')), may hold values from -6 to 6
- upstream: bfloat16 [4096, 8192], P(('seq', 'head')), may hold values from -96 to 96
- send_rows: int32 [8, 768], P('seq'), may hold values from -1 to 511, as said below
- recv_rows: int32 [8, 512], P('seq'), may hold values from 0 to 767, as said below
- doc_lengths: int32 [8, 4], P('seq'), may hold values from 1 to 256, 512 in all within a row
- pair_docs: int32 [32], replicated, may hold values from 0 to 31, each once
- response_mask: int32 [4096], P('seq'), may hold values 0 or 1
- policy_logp: float32 [4096], P('seq'), may hold values from -2.5 to -0.05
- ref_logp: float32 [4096], P('seq'), may hold values from -2.5 to -0.05
Outputs:
- grad_queries: bfloat16 [4096, 8192], P(('seq', 'head'))
- key_row_gradient: bfloat16 [4096, 1024], P(('seq', 'head'))
- value_row_gradient: bfloat16 [4096, 1024], P(('seq', 'head'))
Inputs may be any that keep to these rules, and one draw needn't show every extreme that they name: `send_rows`: entry o * 96 + k of loader group s names the row (of its 512) that owner group o takes as its k-th row from s, or -1 for an empty slot. Every row of a loader group is named exactly once; in each block of 96 entries the named rows come first; every loader group fills some block completely. `recv_rows`: entry p of owner group o names the received slot s * 96 + k (k-th slot from loader group s) that holds its row p. The named slots of an owner group are distinct and are exactly the filled ones. `doc_lengths`: row o lists the lengths of owner group o's 4 dialogues in the order in which they fill its 512 rows; each row sums to 512. Dialogue j of owner group o has the number o * 4 + j. Pair k is the chosen dialogue pair_docs[2k] and the rejected dialogue pair_docs[2k+1]. `response_mask`: 1 marks a response token.
All inputs are finite; a program needn't handle non-finite values. No bound on the sum of `response_mask` on one device may be relied on, other than what follows from the above.
Results may differ from a plain program's by a relative error of at most 0.0088.
Values may be sent and summed in bfloat16 or wider, within the bound.
A program may use at most 128 MiB of HBM per device.

v0:
```python
import functools
import math

import jax
import jax.numpy as jnp
from jax import lax
from jax.experimental import pallas as pl
from jax.experimental.pallas import tpu as pltpu
from jax.sharding import PartitionSpec as P

HEAD_SIZE = 128
DPO_BETA = 0.1
F32 = jnp.float32
BF16 = jnp.bfloat16
VMEM_BYTES = 56 * 1024 * 1024

ROWS_ROWS = (((1,), (1,)), ((), ()))
COLS_COLS = (((0,), (0,)), ((), ()))


def matmul(left, right, dims=(((1,), (0,)), ((), ()))):
    return lax.dot_general(left, right, dims, preferred_element_type=F32)


def attention_kernel(
    cap,
    per_shared,
    kv_here,
    row_info_ref,
    send_cols_ref,
    send_row_ref,
    query_ref,
    upstream_ref,
    kv_ref,
    grad_query_ref,
    grad_kv_ref,
    grad_slots,
):
    owner = pl.program_id(0)
    owners = pl.num_programs(0)
    group_rows = query_ref.shape[0]
    sources = kv_ref.shape[0]
    slot_count = sources * cap
    kv_columns = kv_ref.shape[-1]
    info = row_info_ref[0]
    recv_row = info[0:1, :]
    local_row = info[1:2, :]
    start_row = info[2:3, :]
    coef_row = info[3:4, :]

    slot_iota = lax.broadcasted_iota(jnp.int32, (slot_count, group_rows), 0).astype(F32)
    slot_to_row = jnp.where(slot_iota == recv_row, 1.0, 0.0).astype(BF16)
    slots = kv_ref[...].reshape(slot_count, kv_columns)
    kv_own = matmul(slot_to_row, slots, COLS_COLS).astype(BF16)

    send_column = jnp.transpose(send_cols_ref[0])[:cap, 0:1]
    lane = lax.broadcasted_iota(jnp.int32, (cap, group_rows), 1).astype(F32)
    pick = jnp.where(lane == send_column, 1.0, 0.0).astype(BF16)
    query_slots = matmul(pick, query_ref[...]).astype(BF16)
    upstream_slots = matmul(pick, upstream_ref[...])

    slot = lax.broadcasted_iota(jnp.int32, (cap, group_rows), 0).astype(F32)
    mine = slot == local_row
    position = jnp.sum(jnp.where(mine, lane, 0.0), axis=1, keepdims=True)
    start = jnp.sum(jnp.where(mine, start_row, 0.0), axis=1, keepdims=True)
    coef = jnp.sum(jnp.where(mine, coef_row, 0.0), axis=1, keepdims=True)
    grad_out = (coef * upstream_slots).astype(BF16)
    allowed = (lane >= start) & (lane <= position)

    score_scale = 1.0 / math.sqrt(HEAD_SIZE)
    exp_scale = score_scale * math.log2(math.e)
    grad_key, grad_value = [], []
    grad_query = []
    for shared in range(kv_here):
        key_block = kv_own[:, shared * HEAD_SIZE : (shared + 1) * HEAD_SIZE]
        value_at = (kv_here + shared) * HEAD_SIZE
        value_block = kv_own[:, value_at : value_at + HEAD_SIZE]
        probs_parts, score_parts, query_parts, out_parts = [], [], [], []
        for member in range(per_shared):
            head = shared * per_shared + member
            columns = slice(head * HEAD_SIZE, (head + 1) * HEAD_SIZE)
            query_block = query_slots[:, columns]
            grad_block = grad_out[:, columns]
            scores = jnp.where(allowed, matmul(query_block, key_block, ROWS_ROWS), -1e30)
            highest = jnp.max(scores, axis=1, keepdims=True)
            lifted = jnp.exp2((scores - highest) * exp_scale)
            probs = lifted * (1.0 / jnp.sum(lifted, axis=1, keepdims=True))
            probs_low = probs.astype(BF16)
            grad_probs = matmul(grad_block, value_block, ROWS_ROWS)
            row_dot = jnp.sum(probs_low.astype(F32) * grad_probs, axis=1, keepdims=True)
            grad_scores = (probs * ((grad_probs - row_dot) * score_scale)).astype(BF16)
            probs_parts.append(probs_low)
            score_parts.append(grad_scores)
            query_parts.append(query_block)
            out_parts.append(grad_block)
        grad_scores = jnp.concatenate(score_parts, axis=0)
        head_query = matmul(grad_scores, key_block).astype(BF16)
        for member in range(per_shared):
            grad_query.append(head_query[member * cap : (member + 1) * cap])
        grad_key.append(matmul(grad_scores, jnp.concatenate(query_parts, axis=0), COLS_COLS))
        grad_value.append(
            matmul(
                jnp.concatenate(probs_parts, axis=0), jnp.concatenate(out_parts, axis=0), COLS_COLS
            )
        )
    grad_slots[pl.ds(pl.multiple_of(owner * cap, 16), cap), :] = jnp.concatenate(grad_query, axis=1)
    grad_own = jnp.concatenate(grad_key + grad_value, axis=1).astype(BF16)
    grad_kv_ref[...] = (
        matmul(slot_to_row, grad_own).astype(BF16).reshape(grad_kv_ref.shape)
    )

    @pl.when(owner == owners - 1)
    def _():
        row = lax.broadcasted_iota(jnp.int32, (group_rows, slot_count), 0).astype(F32)
        place = jnp.where(row == send_row_ref[0:1, :], 1.0, 0.0).astype(BF16)
        grad_query_ref[...] = matmul(place, grad_slots[...]).astype(BF16)


def attention(cap, per_shared, kv_here, row_info, send_cols, send_row, query, upstream, kv_slots):
    owners = row_info.shape[0]
    group_rows, columns = query.shape
    slot_count = owners * cap
    kv_columns = kv_slots.shape[-1]
    whole = lambda array: pl.BlockSpec(array.shape, lambda i: (0,) * array.ndim)
    kv_spec = pl.BlockSpec((owners, None, cap, kv_columns), lambda i: (0, i, 0, 0))
    return pl.pallas_call(
        functools.partial(attention_kernel, cap, per_shared, kv_here),
        grid=(owners,),
        in_specs=[
            pl.BlockSpec((1,) + row_info.shape[1:], lambda i: (i, 0, 0)),
            pl.BlockSpec((1,) + send_cols.shape[1:], lambda i: (i, 0, 0)),
            whole(send_row),
            whole(query),
            whole(upstream),
            kv_spec,
        ],
        out_specs=[whole(query), kv_spec],
        out_shape=[
            jax.ShapeDtypeStruct(query.shape, BF16),
            jax.ShapeDtypeStruct(kv_slots.shape, BF16),
        ],
        scratch_shapes=[pltpu.VMEM((slot_count, columns), BF16)],
        compiler_params=pltpu.CompilerParams(vmem_limit_bytes=VMEM_BYTES),
        name="attention_grads",
    )(row_info, send_cols, send_row, query, upstream, kv_slots)


def mesh_place():
    return lax.axis_index("seq"), lax.axis_index("head")


def ring_place(index, size):
    half = size // 2
    up, side = index // 2, index % 2
    return up + side * (2 * half - 1 - 2 * up)


def ring_index(place, size):
    half = size // 2
    side = place // half
    up = place + side * (2 * half - 1 - 2 * place)
    return up * 2 + side


def remote(src, dst, send_sem, recv_sem, seq, head):
    return pltpu.make_async_remote_copy(
        src_ref=src,
        dst_ref=dst,
        send_sem=send_sem,
        recv_sem=recv_sem,
        device_id=(seq, head),
        device_id_type=pl.DeviceIdType.MESH,
    )


def greet(seq, head, seq_peers, heads):
    barrier = pltpu.get_barrier_semaphore()
    for peer in seq_peers:
        pl.semaphore_signal(
            barrier, inc=1, device_id=(peer, head), device_id_type=pl.DeviceIdType.MESH
        )
    for away in range(1, heads):
        pl.semaphore_signal(
            barrier,
            inc=1,
            device_id=(seq, lax.rem(head + away, heads)),
            device_id_type=pl.DeviceIdType.MESH,
        )
    pl.semaphore_wait(barrier, len(seq_peers) + heads - 1)


def gather_kernel(
    owners,
    heads,
    query_in,
    upstream_in,
    key_in,
    value_in,
    facts_in,
    query_out,
    upstream_out,
    kv_out,
    facts_out,
    local_sem,
    head_send,
    head_recv,
    facts_send,
    facts_recv,
    ring_send,
    ring_recv,
):
    seq, head = mesh_place()
    tok = query_in.shape[0]
    wide = query_out.shape[1]
    narrow = kv_out.shape[2] // 2
    group_rows = kv_out.shape[1]
    greet(seq, head, [lax.rem(seq + away, owners) for away in range(1, owners)], heads)

    rows = pl.ds(pl.multiple_of(head * tok, tok), tok)

    def columns(peer, width):
        return pl.ds(pl.multiple_of(peer * width, width), width)

    items = [
        (key_in, kv_out.at[seq, rows, pl.ds(0, narrow)], narrow),
        (value_in, kv_out.at[seq, rows, pl.ds(narrow, narrow)], narrow),
        (query_in, query_out.at[rows], wide),
        (upstream_in, upstream_out.at[rows], wide),
    ]
    locals_, sends = [], []
    for item, (src, dst, width) in enumerate(items):
        copy = pltpu.make_async_copy(src.at[:, columns(head, width)], dst, local_sem.at[item])
        copy.start()
        locals_.append(copy)
        for away in range(1, heads):
            peer = lax.rem(head + away, heads)
            copy = remote(
                src.at[:, columns(peer, width)],
                dst,
                head_send.at[item, away - 1],
                head_recv.at[item, away - 1],
                seq,
                peer,
            )
            copy.start()
            sends.append((item, copy))
    fact_copy = pltpu.make_async_copy(facts_in, facts_out.at[seq], local_sem.at[len(items)])
    fact_copy.start()
    fact_sends = []
    for away in range(1, owners):
        copy = remote(
            facts_in,
            facts_out.at[seq],
            facts_send.at[away - 1],
            facts_recv.at[away - 1],
            lax.rem(seq + away, owners),
            head,
        )
        copy.start()
        fact_sends.append(copy)

    locals_[0].wait()
    locals_[1].wait()
    for item, copy in sends:
        if item < 2:
            copy.wait_recv()

    place = ring_place(seq, owners)
    right = ring_index(lax.rem(place + 1, owners), owners)
    left = ring_index(lax.rem(place + owners - 1, owners), owners)
    part = group_rows // 2
    full = (owners - 1) // 2
    last = {}
    ring = []
    for step in range(owners // 2):
        for chunk in range(2):
            for way in range(2):
                if step == full and chunk != way:
                    continue
                if step > 0:
                    last.pop((way, chunk)).wait_recv()
                if way == 0:
                    shard = ring_index(lax.rem(place + owners - step, owners), owners)
                else:
                    shard = ring_index(lax.rem(place + step, owners), owners)
                block = kv_out.at[shard, pl.ds(chunk * part, part)]
                copy = remote(
                    block,
                    block,
                    ring_send.at[way, step, chunk],
                    ring_recv.at[way, step, chunk],
                    right if way == 0 else left,
                    head,
                )
                copy.start()
                last[(way, chunk)] = copy
                ring.append(copy)
    for copy in last.values():
        copy.wait_recv()
    for item, copy in sends:
        if item >= 2:
            copy.wait_recv()
    for copy in fact_sends:
        copy.wait_recv()
    locals_[2].wait()
    locals_[3].wait()
    fact_copy.wait()
    for copy in [c for _, c in sends] + fact_sends + ring:
        copy.wait_send()


def gather(owners, heads, queries, upstream, keys, values, facts):
    tok = queries.shape[0]
    group_rows = tok * heads
    group = jax.ShapeDtypeStruct((group_rows, queries.shape[1] // heads), BF16)
    kv = jax.ShapeDtypeStruct((owners, group_rows, 2 * keys.shape[1] // heads), BF16)
    dma = pltpu.SemaphoreType.DMA
    anywhere = pl.BlockSpec(memory_space=pl.ANY)
    return pl.pallas_call(
        functools.partial(gather_kernel, owners, heads),
        in_specs=[anywhere] * 5,
        out_specs=[anywhere] * 4,
        out_shape=[group, group, kv, jax.ShapeDtypeStruct((owners,) + facts.shape, F32)],
        scratch_shapes=[
            dma((5,)),
            dma((4, heads - 1)),
            dma((4, heads - 1)),
            dma((owners - 1,)),
            dma((owners - 1,)),
            dma((2, owners // 2, 2)),
            dma((2, owners // 2, 2)),
        ],
        compiler_params=pltpu.CompilerParams(
            collective_id=0, has_side_effects=True, vmem_limit_bytes=VMEM_BYTES
        ),
        name="gather_rows",
    )(queries, upstream, keys, values, facts)


def scatter_kernel(
    owners,
    heads,
    send_ref,
    slots_ref,
    query_in,
    query_out,
    key_out,
    value_out,
    sums,
    final,
    local_sem,
    head_send,
    head_recv,
    ring_send,
    ring_recv,
):
    seq, head = mesh_place()
    tok = query_out.shape[0]
    wide = query_in.shape[1]
    group_rows = query_in.shape[0]
    narrow = slots_ref.shape[2] // 2
    slot_count = slots_ref.shape[1]
    part = group_rows // 2
    place = ring_place(seq, owners)
    right = ring_index(lax.rem(place + 1, owners), owners)
    left = ring_index(lax.rem(place + owners - 1, owners), owners)
    greet(seq, head, [right, left], heads)

    def rows_of(peer):
        return pl.ds(pl.multiple_of(peer * tok, tok), tok)

    def exchange(item, src, dst, width):
        mine = dst.at[:, pl.ds(pl.multiple_of(head * width, width), width)]
        local = pltpu.make_async_copy(src.at[rows_of(head)], mine, local_sem.at[item])
        local.start()
        sends = []
        for away in range(1, heads):
            peer = lax.rem(head + away, heads)
            copy = remote(
                src.at[rows_of(peer)],
                mine,
                head_send.at[item, away - 1],
                head_recv.at[item, away - 1],
                seq,
                peer,
            )
            copy.start()
            sends.append(copy)
        return local, sends

    moved = [exchange(0, query_in, query_out, wide)]

    def shard_of(way, step):
        if way == 0:
            return ring_index(lax.rem(place + 2 * owners - 1 - step, owners), owners)
        return ring_index(lax.rem(place + 1 + step, owners), owners)

    def partial_sum(way, step, chunk):
        shard = shard_of(way, step)
        row = lax.broadcasted_iota(jnp.int32, (part, slot_count), 0).astype(F32) + float(chunk * part)
        spread = jnp.where(row == send_ref[shard], 1.0, 0.0).astype(BF16)
        return matmul(spread, slots_ref[shard, :, way * narrow : (way + 1) * narrow])

    def hop(way, step, chunk):
        return remote(
            sums.at[way, step, chunk],
            sums.at[way, step + 1, chunk],
            ring_send.at[way, step, chunk],
            ring_recv.at[way, step, chunk],
            right if way == 0 else left,
            head,
        )

    every = [(way, chunk) for chunk in range(2) for way in range(2)]
    for way, chunk in every:
        sums[way, 0, chunk] = partial_sum(way, 0, chunk).astype(BF16)
        hop(way, 0, chunk).start()

    def one_step(step, carry):
        for way, chunk in every:
            own = partial_sum(way, step, chunk)
            hop(way, step - 1, chunk).wait_recv()
            sums[way, step, chunk] = (own + sums[way, step, chunk].astype(F32)).astype(BF16)
            hop(way, step, chunk).start()
        return carry

    lax.fori_loop(1, owners - 1, one_step, 0)
    for way in range(2):
        for chunk in range(2):
            own = partial_sum(way, owners - 1, chunk)
            hop(way, owners - 2, chunk).wait_recv()
            total = own + sums[way, owners - 1, chunk].astype(F32)
            final[way, chunk * part : (chunk + 1) * part] = total.astype(BF16)
        moved.append(exchange(1 + way, final.at[way], key_out if way == 0 else value_out, narrow))

    def drain(step, carry):
        for way, chunk in every:
            hop(way, step, chunk).wait_send()
        return carry

    lax.fori_loop(0, owners - 1, drain, 0)
    for local, sends in moved:
        local.wait()
        for copy in sends:
            copy.wait()


def scatter(owners, heads, send_all, grad_slots, grad_query):
    group_rows, wide = grad_query.shape
    narrow = grad_slots.shape[2] // 2
    tok = group_rows // heads
    dma = pltpu.SemaphoreType.DMA
    anywhere = pl.BlockSpec(memory_space=pl.ANY)
    vmem = pl.BlockSpec(memory_space=pltpu.VMEM)
    return pl.pallas_call(
        functools.partial(scatter_kernel, owners, heads),
        in_specs=[vmem, vmem, anywhere],
        out_specs=[anywhere] * 3,
        out_shape=[
            jax.ShapeDtypeStruct((tok, wide * heads), BF16),
            jax.ShapeDtypeStruct((tok, narrow * heads), BF16),
            jax.ShapeDtypeStruct((tok, narrow * heads), BF16),
        ],
        scratch_shapes=[
            pltpu.VMEM((2, owners, 2, group_rows // 2, narrow), BF16),
            pltpu.VMEM((2, group_rows, narrow), BF16),
            dma((3,)),
            dma((3, heads - 1)),
            dma((3, heads - 1)),
            dma((2, owners - 1, 2)),
            dma((2, owners - 1, 2)),
        ],
        compiler_params=pltpu.CompilerParams(
            collective_id=1, has_side_effects=True, vmem_limit_bytes=VMEM_BYTES
        ),
        name="scatter_grads",
    )(send_all, grad_slots, grad_query)


def pair_coefficients(doc_gap, pair_docs):
    docs = jnp.arange(doc_gap.shape[0], dtype=jnp.int32)
    chosen = pair_docs[0::2][:, None] == docs[None, :]
    rejected = pair_docs[1::2][:, None] == docs[None, :]
    sign = chosen.astype(F32) - rejected.astype(F32)
    margin = DPO_BETA * jnp.sum(sign * doc_gap[None, :], axis=1)
    weight = DPO_BETA * jax.nn.sigmoid(-margin)
    return -jnp.sum(sign * weight[:, None], axis=0)


def body(
    queries,
    keys,
    values,
    upstream,
    send_rows,
    recv_rows,
    doc_lengths,
    pair_docs,
    response_mask,
    policy_logp,
    ref_logp,
):
    tok_rows = queries.shape[0]
    head_devices = lax.axis_size("head")
    owners = lax.axis_size("seq")
    group_rows = tok_rows * head_devices
    slot_count = send_rows.shape[1]
    cap = slot_count // owners
    kv_heads = keys.shape[1] // HEAD_SIZE
    kv_here = kv_heads // head_devices
    per_shared = queries.shape[1] // keys.shape[1]

    doc_len = doc_lengths[0]
    doc_count = doc_len.shape[0]
    doc_ends = jnp.cumsum(doc_len)
    position = jnp.arange(group_rows, dtype=jnp.int32)
    doc_of_row = jnp.sum((position[:, None] >= doc_ends[None, :]).astype(jnp.int32), axis=1)
    member = doc_of_row[:, None] == jnp.arange(doc_count, dtype=jnp.int32)[None, :]
    token_gap = response_mask.astype(F32) * (policy_logp - ref_logp)
    doc_gap = jnp.sum(jnp.where(member, token_gap[:, None], 0.0), axis=0)
    facts = jnp.concatenate(
        [send_rows[0].astype(F32), recv_rows[0].astype(F32), doc_len.astype(F32), doc_gap]
    )
    facts = jnp.pad(facts, (0, -facts.shape[0] % 1024)).reshape(-1, 128)
    query_group, upstream_group, kv_all, facts = gather(
        owners, head_devices, queries, upstream, keys, values, facts
    )
    facts = facts.reshape(owners, -1)

    send_all = facts[:, :slot_count]
    recv_all = facts[:, slot_count : slot_count + group_rows]
    at = slot_count + group_rows
    len_all = facts[:, at : at + doc_count]
    gap_all = facts[:, at + doc_count : at + 2 * doc_count]
    doc_coef = pair_coefficients(gap_all.reshape(-1), pair_docs).reshape(owners, doc_count)
    ends = jnp.cumsum(len_all, axis=1)
    starts = ends - len_all
    place = jnp.arange(group_rows, dtype=jnp.int32).astype(F32)
    inside = (place[None, :, None] >= starts[:, None, :]) & (place[None, :, None] < ends[:, None, :])
    start_of_row = jnp.sum(jnp.where(inside, starts[:, None, :], 0.0), axis=2)
    coef_of_row = jnp.sum(jnp.where(inside, doc_coef[:, None, :], 0.0), axis=2)
    first_slot = (lax.axis_index("seq") * cap).astype(F32)
    zero = jnp.zeros_like(recv_all)
    row_info = jnp.stack(
        [recv_all, recv_all - first_slot, start_of_row, coef_of_row, zero, zero, zero, zero], axis=1
    )
    own_send = send_rows[0].astype(F32)
    send_cols = jnp.pad(
        own_send.reshape(owners, 1, cap), ((0, 0), (0, 7), (0, -cap % 128)), constant_values=-1.0
    )
    send_row = jnp.broadcast_to(own_send[None, :], (8, slot_count))

    row = jnp.arange(group_rows, dtype=jnp.int32).astype(F32)
    slot_of_row = (send_all[:, :, None] == row[None, None, :]).astype(BF16)
    kv_slots = jnp.einsum("sjr,src->sjc", slot_of_row, kv_all, preferred_element_type=F32)
    kv_slots = kv_slots.astype(BF16).reshape(owners, owners, cap, -1)

    grad_query, grad_slots = attention(
        cap,
        per_shared,
        kv_here,
        row_info,
        send_cols,
        send_row,
        query_group,
        upstream_group,
        kv_slots,
    )

    grad_slots = grad_slots.reshape(owners, slot_count, -1)
    return tuple(
        scatter(owners, head_devices, send_all[:, None, :], grad_slots, grad_query)
    )


def solution(mesh):
    rows = P(("seq", "head"), None)
    return jax.shard_map(
        body,
        mesh=mesh,
        in_specs=(
            rows,
            rows,
            rows,
            rows,
            P("seq", None),
            P("seq", None),
            P("seq", None),
            P(),
            P("seq"),
            P("seq"),
            P("seq"),
        ),
        out_specs=(rows, rows, rows),
        check_vma=False,
    )
```

profile of v0, /device:TPU:0, one launch (start us, length us, event | category | flops | bytes accessed | tf_op | source)
XLA Modules:
  0.0 183.2 jit_solution(6602047434926256711)
XLA Ops:
  0.6 0.8 slice.22
  1.4 0.8 slice.21
  2.1 0.8 reduce-window.8
  3.0 0.7 convert_bitcast_fusion
  3.6 0.1 convert_reduce_fusion
  3.7 0.7 convert_element_type.69
  4.4 0.7 subtract_multiply_fusion
  5.1 0.1 select_reduce_fusion.2
  5.2 0.7 convert_reduce_fusion.1
  5.9 0.1 convert_element_type.79
  6.1 0.6 pad_bitcast_fusion.facts_in
  6.7 0.6 broadcast_in_dim.37.send_row_ref
  7.3 0.6 pad.9.send_cols_ref
  7.9 57.5 %gather_rows.1 = (bf16[512,2048]{1,0:T(8,128)(2,1)}, bf16[512,2048]{1,0:T(8,128)(2,1)}, bf16[8,512,512]{2,1,0:T(8,128)(2,1)}, f32[8,16,128]{2,1,0:T(8,128)}) custom-call(bf16[128,8192]{1,0:T(8,128)(2,1)} %query_in.1, bf16[128,8192]{1,0:T(8,128)(2,1)} %upstream_in.1, bf16[128,1024]{1,0:T(8,128)(2,1)} %key_in.1, bf16[128,1024]{1,0:T(8,128)(2,1)} %value_in.1, ...), custom_call_target="tpu_custom_call" | custom-call | tf_op jit(solution)/shard_map/gather_rows/pallas_call | solution.py:319
  65.5 0.9 copy.25
  66.3 0.2 reduce_window_sum.18
  66.5 0.1 copy.19
  66.7 0.1 copy.18
  66.7 0.1 mul.40
  66.8 0.2 multiply_reduce_fusion.1
  67.0 0.1 multiply_reduce_fusion
  67.1 0.1 neg.13
  67.2 0.1 copy.20
  67.4 0.6 broadcast_in_dim.34.send_ref
  68.0 0.1 select_reduce_fusion
  68.1 0.8 stack.23.row_info_ref
  68.9 7.6 %fusion.4 = bf16[8,768,512]{2,1,0:T(8,128)(2,1)} fusion(bf16[8,512,512]{2,1,0:T(8,128)(2,1)} %get-tuple-element.12, f32[512]{0:T(512)S(1)} %iota_convert_fusion, f32[8,768]{1,0:T(8,128)S(1)} %slice.24), kind=kOutput, calls=%fused_computation.4 | convolution fusion | flops 3227516928 | bytes 10512384 | tf_op jit(solution)/shard_map/sjr,src->sjc/dot_general | solution.py:555
  76.5 48.4 %attention_grads.1 = (bf16[512,2048]{1,0:T(8,128)(2,1)}, bf16[8,8,96,512]{3,2,1,0:T(8,128)(2,1)}) custom-call(f32[8,8,512]{2,1,0:T(8,128)} %stack.23.row_info_ref, f32[8,8,128]{2,1,0:T(8,128)} %pad.9.send_cols_ref, f32[8,768]{1,0:T(8,128)} %broadcast_in_dim.37.send_row_ref, bf16[512,2048]{1,0:T(8,128)(2,1)} %get-tuple-element.10.query_ref, ...), custom_call_target="tpu_custom_call" | custom-call | tf_op jit(solution)/shard_map/attention_grads/pallas_call | solution.py:126
  124.8 53.8 %scatter_grads.1 = (bf16[128,8192]{1,0:T(8,128)(2,1)}, bf16[128,1024]{1,0:T(8,128)(2,1)}, bf16[128,1024]{1,0:T(8,128)(2,1)}) custom-call(f32[8,1,768]{2,1,0:T(1,128)} %broadcast_in_dim.34.send_ref, bf16[8,768,512]{2,1,0:T(8,128)(2,1)} %bitcast.18, bf16[512,2048]{1,0:T(8,128)(2,1)} %get-tuple-element.14.query_in), custom_call_target="tpu_custom_call" | custom-call | tf_op jit(solution)/shard_map/scatter_grads/pallas_call | solution.py:455
  178.6 3.2 %copy.29 = bf16[128,8192]{1,0:T(8,128)(2,1)} copy(bf16[128,8192]{1,0:T(8,128)(2,1)} %get-tuple-element.24) | data formatting | bytes 4194304
  181.8 0.7 copy.30
  182.5 0.7 copy.31
  (17 shorter events, 0.3 us)
Async XLA Ops:
  178.6 3.2 %copy-start.1 = (bf16[128,1024]{1,0:T(8,128)(2,1)S(1)}, bf16[128,1024]{1,0:T(8,128)(2,1)}, u32[]{:S(2)}) copy-start(bf16[128,1024]{1,0:T(8,128)(2,1)} %get-tuple-element.25) | copy-start | bytes 786436
  178.6 3.9 %copy-start = (bf16[128,1024]{1,0:T(8,128)(2,1)S(1)}, bf16[128,1024]{1,0:T(8,128)(2,1)}, u32[]{:S(2)}) copy-start(bf16[128,1024]{1,0:T(8,128)(2,1)} %get-tuple-element.26) | copy-start | bytes 786436
where the time goes:
time: 184 us; the launch traced here: 183 us
  Pallas kernels  160 us (87%)
  local copies, waits for them, and re-layouts  10.8 us (6%)
  matrix products  7.58 us (4%)
  other arithmetic  4.4 us (2%)
    pallas_call x1, Pallas kernels, gather(): pl.pallas_call(functools.partial(gather_kernel, owners, heads), in_specs=...  57.5 us
    pallas_call x1, Pallas kernels, scatter(): pl.pallas_call(functools.partial(scatter_kernel, owners, heads), in_specs...  53.8 us
    pallas_call x1, Pallas kernels, attention(): pl.pallas_call(functools.partial(attention_kernel, cap, per_shared, kv_he...  48.4 us
    dot_general x1, matrix products, body(): jnp.einsum('sjr,src->sjc', slot_of_row, kv_all, preferred_element_type=F32)  7.58 us
    unnamed x8, local copies, waits for them, and re-layouts  5.43 us

commit v1 on v0

--- a/solution.py
+++ b/solution.py
@@ -45,64 +45,73 @@
     info = row_info_ref[0]
     recv_row = info[0:1, :]
     local_row = info[1:2, :]
-    start_row = info[2:3, :]
     coef_row = info[3:4, :]
 
-    slot_iota = lax.broadcasted_iota(jnp.int32, (slot_count, group_rows), 0).astype(F32)
-    slot_to_row = jnp.where(slot_iota == recv_row, 1.0, 0.0).astype(BF16)
+    columns_of = jnp.transpose(info)
+    recv_column = columns_of[:, 0:1]
+    local_column = columns_of[:, 1:2]
+    start_column = columns_of[:, 2:3]
+
+    slot_lane = lax.broadcasted_iota(jnp.int32, (group_rows, slot_count), 1).astype(F32)
+    row_to_slot = jnp.where(slot_lane == recv_column, 1.0, 0.0).astype(BF16)
     slots = kv_ref[...].reshape(slot_count, kv_columns)
-    kv_own = matmul(slot_to_row, slots, COLS_COLS).astype(BF16)
+    kv_own = matmul(row_to_slot, slots).astype(BF16)
 
     send_column = jnp.transpose(send_cols_ref[0])[:cap, 0:1]
     lane = lax.broadcasted_iota(jnp.int32, (cap, group_rows), 1).astype(F32)
     pick = jnp.where(lane == send_column, 1.0, 0.0).astype(BF16)
     query_slots = matmul(pick, query_ref[...]).astype(BF16)
     upstream_slots = matmul(pick, upstream_ref[...])
-
     slot = lax.broadcasted_iota(jnp.int32, (cap, group_rows), 0).astype(F32)
-    mine = slot == local_row
-    position = jnp.sum(jnp.where(mine, lane, 0.0), axis=1, keepdims=True)
-    start = jnp.sum(jnp.where(mine, start_row, 0.0), axis=1, keepdims=True)
-    coef = jnp.sum(jnp.where(mine, coef_row, 0.0), axis=1, keepdims=True)
+    coef = jnp.sum(jnp.where(slot == local_row, coef_row, 0.0), axis=1, keepdims=True)
     grad_out = (coef * upstream_slots).astype(BF16)
-    allowed = (lane >= start) & (lane <= position)
+
+    across = lax.broadcasted_iota(jnp.int32, (group_rows, cap), 1).astype(F32)
+    down = lax.broadcasted_iota(jnp.int32, (group_rows, cap), 0).astype(F32)
+    mine = across == local_column
+    position = jnp.sum(jnp.where(mine, down, 0.0), axis=0, keepdims=True)
+    start = jnp.sum(jnp.where(mine, start_column, 0.0), axis=0, keepdims=True)
+    stacked = per_shared * cap
+    position = jnp.concatenate([position] * per_shared, axis=1)
+    start = jnp.concatenate([start] * per_shared, axis=1)
+    key_row = lax.broadcasted_iota(jnp.int32, (group_rows, stacked), 0).astype(F32)
+    bias = jnp.where((key_row >= start) & (key_row <= position), 0.0, -1e30)
 
     score_scale = 1.0 / math.sqrt(HEAD_SIZE)
     exp_scale = score_scale * math.log2(math.e)
+    width = next((w for w in (256, 128) if stacked % w == 0), stacked)
     grad_key, grad_value = [], []
     grad_query = []
     for shared in range(kv_here):
         key_block = kv_own[:, shared * HEAD_SIZE : (shared + 1) * HEAD_SIZE]
         value_at = (kv_here + shared) * HEAD_SIZE
         value_block = kv_own[:, value_at : value_at + HEAD_SIZE]
-        probs_parts, score_parts, query_parts, out_parts = [], [], [], []
-        for member in range(per_shared):
-            head = shared * per_shared + member
-            columns = slice(head * HEAD_SIZE, (head + 1) * HEAD_SIZE)
-            query_block = query_slots[:, columns]
-            grad_block = grad_out[:, columns]
-            scores = jnp.where(allowed, matmul(query_block, key_block, ROWS_ROWS), -1e30)
-            highest = jnp.max(scores, axis=1, keepdims=True)
+        heads = [
+            slice(head * HEAD_SIZE, (head + 1) * HEAD_SIZE)
+            for head in range(shared * per_shared, (shared + 1) * per_shared)
+        ]
+        queries = jnp.concatenate([query_slots[:, head] for head in heads], axis=0)
+        grads = jnp.concatenate([grad_out[:, head] for head in heads], axis=0)
+        probs_parts, score_parts = [], []
+        for at in range(0, stacked, width):
+            scores = matmul(key_block, queries[at : at + width], ROWS_ROWS)
+            scores = scores + bias[:, at : at + width]
+            highest = jnp.max(scores, axis=0, keepdims=True)
             lifted = jnp.exp2((scores - highest) * exp_scale)
-            probs = lifted * (1.0 / jnp.sum(lifted, axis=1, keepdims=True))
+            probs = lifted * (1.0 / jnp.sum(lifted, axis=0, keepdims=True))
             probs_low = probs.astype(BF16)
-            grad_probs = matmul(grad_block, value_block, ROWS_ROWS)
-            row_dot = jnp.sum(probs_low.astype(F32) * grad_probs, axis=1, keepdims=True)
-            grad_scores = (probs * ((grad_probs - row_dot) * score_scale)).astype(BF16)
+            grad_probs = matmul(value_block, grads[at : at + width], ROWS_ROWS)
+            row_dot = jnp.sum(probs_low.astype(F32) * grad_probs, axis=0, keepdims=True)
             probs_parts.append(probs_low)
-            score_parts.append(grad_scores)
-            query_parts.append(query_block)
-            out_parts.append(grad_block)
-        grad_scores = jnp.concatenate(score_parts, axis=0)
-        head_query = matmul(grad_scores, key_block).astype(BF16)
+            score_parts.append((probs * ((grad_probs - row_dot) * score_scale)).astype(BF16))
+        grad_scores = jnp.concatenate(score_parts, axis=1)
+        head_query = matmul(grad_scores, key_block, COLS_COLS).astype(BF16)
         for member in range(per_shared):
             grad_query.append(head_query[member * cap : (member + 1) * cap])
-        grad_key.append(matmul(grad_scores, jnp.concatenate(query_parts, axis=0), COLS_COLS))
-        grad_value.append(
-            matmul(
-                jnp.concatenate(probs_parts, axis=0), jnp.concatenate(out_parts, axis=0), COLS_COLS
-            )
-        )
+        grad_key.append(matmul(grad_scores, queries))
+        grad_value.append(matmul(jnp.concatenate(probs_parts, axis=1), grads))
+    slot_down = lax.broadcasted_iota(jnp.int32, (slot_count, group_rows), 0).astype(F32)
+    slot_to_row = jnp.where(slot_down == recv_row, 1.0, 0.0).astype(BF16)
     grad_slots[pl.ds(pl.multiple_of(owner * cap, 16), cap), :] = jnp.concatenate(grad_query, axis=1)
     grad_own = jnp.concatenate(grad_key + grad_value, axis=1).astype(BF16)
     grad_kv_ref[...] = (
@@ -199,8 +208,9 @@
     facts_in,
     query_out,
     upstream_out,
+    slots_out,
+    facts_out,
     kv_out,
-    facts_out,
     local_sem,
     head_send,
     head_recv,
@@ -228,7 +238,27 @@
         (upstream_in, upstream_out.at[rows], wide),
     ]
     locals_, sends = [], []
+    fact_sends = []
+
+    def send_facts():
+        fact_copy = pltpu.make_async_copy(facts_in, facts_out.at[seq], local_sem.at[len(items)])
+        fact_copy.start()
+        for away in range(1, owners):
+            copy = remote(
+                facts_in,
+                facts_out.at[seq],
+                facts_send.at[away - 1],
+                facts_recv.at[away - 1],
+                lax.rem(seq + away, owners),
+                head,
+            )
+            copy.start()
+            fact_sends.append(copy)
+        return fact_copy
+
     for item, (src, dst, width) in enumerate(items):
+        if item == 2:
+            fact_copy = send_facts()
         copy = pltpu.make_async_copy(src.at[:, columns(head, width)], dst, local_sem.at[item])
         copy.start()
         locals_.append(copy)
@@ -244,21 +274,6 @@
             )
             copy.start()
             sends.append((item, copy))
-    fact_copy = pltpu.make_async_copy(facts_in, facts_out.at[seq], local_sem.at[len(items)])
-    fact_copy.start()
-    fact_sends = []
-    for away in range(1, owners):
-        copy = remote(
-            facts_in,
-            facts_out.at[seq],
-            facts_send.at[away - 1],
-            facts_recv.at[away - 1],
-            lax.rem(seq + away, owners),
-            head,
-        )
-        copy.start()
-        fact_sends.append(copy)
-
     locals_[0].wait()
     locals_[1].wait()
     for item, copy in sends:
@@ -270,58 +285,90 @@
     left = ring_index(lax.rem(place + owners - 1, owners), owners)
     part = group_rows // 2
     full = (owners - 1) // 2
-    last = {}
-    ring = []
-    for step in range(owners // 2):
-        for chunk in range(2):
-            for way in range(2):
-                if step == full and chunk != way:
-                    continue
-                if step > 0:
-                    last.pop((way, chunk)).wait_recv()
-                if way == 0:
-                    shard = ring_index(lax.rem(place + owners - step, owners), owners)
-                else:
-                    shard = ring_index(lax.rem(place + step, owners), owners)
-                block = kv_out.at[shard, pl.ds(chunk * part, part)]
-                copy = remote(
-                    block,
-                    block,
-                    ring_send.at[way, step, chunk],
-                    ring_recv.at[way, step, chunk],
-                    right if way == 0 else left,
-                    head,
-                )
-                copy.start()
-                last[(way, chunk)] = copy
-                ring.append(copy)
-    for copy in last.values():
+    slot_count = slots_out.shape[1]
+    every = [(way, chunk) for chunk in range(2) for way in range(2)]
+    half_way = [(0, 0), (1, 1)] if owners % 2 == 0 else []
+
+    def shard_at(way, step):
+        return ring_index(lax.rem(place + (owners - step if way == 0 else step), owners), owners)
+
+    def hop(way, step, chunk):
+        block = kv_out.at[shard_at(way, step), pl.ds(chunk * part, part)]
+        return remote(
+            block,
+            block,
+            ring_send.at[way, step, chunk],
+            ring_recv.at[way, step, chunk],
+            right if way == 0 else left,
+            head,
+        )
+
+    def pack(shard):
+        row = lax.broadcasted_iota(jnp.int32, (group_rows, slot_count), 0).astype(F32)
+        send_row = facts_out[shard, 0:1, 0:slot_count]
+        spread = jnp.where(row == send_row, 1.0, 0.0).astype(BF16)
+        slots_out[shard] = matmul(spread, kv_out[shard], COLS_COLS).astype(BF16)
+
+    for way, chunk in every:
+        hop(way, 0, chunk).start()
+    fact_copy.wait()
+    for copy in fact_sends:
         copy.wait_recv()
+    pack(seq)
+
+    def one_step(step, carry):
+        for way, chunk in every:
+            hop(way, step - 1, chunk).wait_recv()
+            hop(way, step, chunk).start()
+        for way in range(2):
+            pack(shard_at(way, step))
+        return carry
+
+    lax.fori_loop(1, full, one_step, 0)
+    for way, chunk in every:
+        hop(way, full - 1, chunk).wait_recv()
+        if (way, chunk) in half_way:
+            hop(way, full, chunk).start()
+    for way in range(2):
+        pack(shard_at(way, full))
+    for way, chunk in half_way:
+        hop(way, full, chunk).wait_recv()
+    if half_way:
+        pack(shard_at(0, full + 1))
+
+    def drain(step, carry):
+        for way, chunk in every:
+            hop(way, step, chunk).wait_send()
+        return carry
+
+    lax.fori_loop(0, full, drain, 0)
+    for way, chunk in half_way:
+        hop(way, full, chunk).wait_send()
+    locals_[2].wait()
+    locals_[3].wait()
     for item, copy in sends:
         if item >= 2:
             copy.wait_recv()
-    for copy in fact_sends:
-        copy.wait_recv()
-    locals_[2].wait()
-    locals_[3].wait()
-    fact_copy.wait()
-    for copy in [c for _, c in sends] + fact_sends + ring:
+    for copy in [c for _, c in sends] + fact_sends:
         copy.wait_send()
 
 
-def gather(owners, heads, queries, upstream, keys, values, facts):
+def gather(owners, heads, slot_count, queries, upstream, keys, values, facts):
     tok = queries.shape[0]
     group_rows = tok * heads
     group = jax.ShapeDtypeStruct((group_rows, queries.shape[1] // heads), BF16)
-    kv = jax.ShapeDtypeStruct((owners, group_rows, 2 * keys.shape[1] // heads), BF16)
+    kv_columns = 2 * keys.shape[1] // heads
+    slots = jax.ShapeDtypeStruct((owners, slot_count, kv_columns), BF16)
     dma = pltpu.SemaphoreType.DMA
     anywhere = pl.BlockSpec(memory_space=pl.ANY)
+    vmem = pl.BlockSpec(memory_space=pltpu.VMEM)
     return pl.pallas_call(
         functools.partial(gather_kernel, owners, heads),
         in_specs=[anywhere] * 5,
-        out_specs=[anywhere] * 4,
-        out_shape=[group, group, kv, jax.ShapeDtypeStruct((owners,) + facts.shape, F32)],
+        out_specs=[anywhere, anywhere, vmem, vmem],
+        out_shape=[group, group, slots, jax.ShapeDtypeStruct((owners,) + facts.shape, F32)],
         scratch_shapes=[
+            pltpu.VMEM((owners, group_rows, kv_columns), BF16),
             dma((5,)),
             dma((4, heads - 1)),
             dma((4, heads - 1)),
@@ -521,11 +568,12 @@
     facts = jnp.concatenate(
         [send_rows[0].astype(F32), recv_rows[0].astype(F32), doc_len.astype(F32), doc_gap]
     )
-    facts = jnp.pad(facts, (0, -facts.shape[0] % 1024)).reshape(-1, 128)
-    query_group, upstream_group, kv_all, facts = gather(
-        owners, head_devices, queries, upstream, keys, values, facts
-    )
-    facts = facts.reshape(owners, -1)
+    facts = jnp.pad(facts, (0, -facts.shape[0] % 128))
+    facts = jnp.broadcast_to(facts[None, :], (8, facts.shape[0]))
+    query_group, upstream_group, kv_slots, facts = gather(
+        owners, head_devices, slot_count, queries, upstream, keys, values, facts
+    )
+    facts = facts[:, 0]
 
     send_all = facts[:, :slot_count]
     recv_all = facts[:, slot_count : slot_count + group_rows]
@@ -550,11 +598,7 @@
     )
     send_row = jnp.broadcast_to(own_send[None, :], (8, slot_count))
 
-    row = jnp.arange(group_rows, dtype=jnp.int32).astype(F32)
-    slot_of_row = (send_all[:, :, None] == row[None, None, :]).astype(BF16)
-    kv_slots = jnp.einsum("sjr,src->sjc", slot_of_row, kv_all, preferred_element_type=F32)
-    kv_slots = kv_slots.astype(BF16).reshape(owners, owners, cap, -1)
-
+    kv_slots = kv_slots.reshape(owners, owners, cap, -1)
     grad_query, grad_slots = attention(
         cap,
         per_shared,

time: 184 us -> 178 us (0.967)
  matrix products: 7.58 us -> 0 us
    dot_general x1 -> x0, matrix products: 7.58 us -> none  [body(): jnp.einsum('sjr,src->sjc', slot_of_row, kv_all, preferred_element_type=F32)]
    pallas_call x1, Pallas kernels: 57.5 us -> 60.3 us  [gather(): pl.pallas_call(functools.partial(gather_kernel, owners, heads), in_specs=...]
    unnamed x8 -> x7, local copies, waits for them, and re-layouts: 5.43 us -> 4.56 us
where the time goes in v1:
time: 178 us
  Pallas kernels  161 us (90%)
  local copies, waits for them, and re-layouts  11 us (6%)
  other arithmetic  4.4 us (2%)
    pallas_call x1, Pallas kernels, gather(): pl.pallas_call(functools.partial(gather_kernel, owners, heads), in_specs=...  60.3 us
    pallas_call x1, Pallas kernels, scatter(): pl.pallas_call(functools.partial(scatter_kernel, owners, heads), in_specs...  53.1 us
    pallas_call x1, Pallas kernels, attention(): pl.pallas_call(functools.partial(attention_kernel, cap, per_shared, kv_he...  47.9 us
    unnamed x7, local copies, waits for them, and re-layouts  4.56 us

profile of v1, /device:TPU:0, one launch (start us, length us, event | category | flops | bytes accessed | tf_op | source)
XLA Modules:
  0.0 177.5 jit_solution(10442392056823341867)
XLA Ops:
  0.6 0.8 slice.26
  1.4 0.8 slice.25
  2.1 0.8 reduce-window.8
  3.0 0.7 convert_bitcast_fusion
  3.6 0.1 convert_reduce_fusion
  3.7 0.7 convert_element_type.58
  4.4 0.7 subtract_multiply_fusion
  5.1 0.1 select_reduce_fusion.2
  5.2 0.7 convert_reduce_fusion.1
  5.9 0.1 convert_element_type.68
  6.0 0.1 concatenate.3
  6.1 0.6 broadcast_in_dim.64.send_row_ref
  6.7 0.6 pad.9.send_cols_ref
  7.3 0.6 broadcast_in_dim.36.facts_in
  8.0 60.3 %gather_rows.1 = (bf16[512,2048]{1,0:T(8,128)(2,1)}, bf16[512,2048]{1,0:T(8,128)(2,1)}, bf16[8,768,512]{2,1,0:T(8,128)(2,1)}, f32[8,8,1408]{2,1,0:T(8,128)}) custom-call(bf16[128,8192]{1,0:T(8,128)(2,1)} %query_in.1, bf16[128,8192]{1,0:T(8,128)(2,1)} %upstream_in.1, bf16[128,1024]{1,0:T(8,128)(2,1)} %key_in.1, bf16[128,1024]{1,0:T(8,128)(2,1)} %value_in.1, ...), custom_call_target="tpu_custom_call" | custom-call | tf_op jit(solution)/shard_map/gather_rows/pallas_call | solution.py:365
  68.3 1.1 copy.20
  69.3 0.2 reduce_window_sum.18
  69.5 0.1 copy.22
  69.7 0.1 copy.21
  69.7 0.1 mul.40
  69.8 0.2 multiply_reduce_fusion.1
  70.0 0.1 multiply_reduce_fusion
  70.1 0.1 neg.13
  70.2 0.1 copy.23
  70.3 0.6 broadcast_in_dim.37.send_ref
  71.0 0.1 select_reduce_fusion
  71.1 0.8 stack.23.row_info_ref
  71.9 47.9 %attention_grads.1 = (bf16[512,2048]{1,0:T(8,128)(2,1)}, bf16[8,8,96,512]{3,2,1,0:T(8,128)(2,1)}) custom-call(f32[8,8,512]{2,1,0:T(8,128)} %stack.23.row_info_ref, f32[8,8,128]{2,1,0:T(8,128)} %pad.9.send_cols_ref, f32[8,768]{1,0:T(8,128)} %broadcast_in_dim.64.send_row_ref, bf16[512,2048]{1,0:T(8,128)(2,1)} %get-tuple-element.10.query_ref, ...), custom_call_target="tpu_custom_call" | custom-call | tf_op jit(solution)/shard_map/attention_grads/pallas_call | solution.py:135
  119.8 53.1 %scatter_grads.1 = (bf16[128,8192]{1,0:T(8,128)(2,1)}, bf16[128,1024]{1,0:T(8,128)(2,1)}, bf16[128,1024]{1,0:T(8,128)(2,1)}) custom-call(f32[8,1,768]{2,1,0:T(1,128)} %broadcast_in_dim.37.send_ref, bf16[8,768,512]{2,1,0:T(8,128)(2,1)} %bitcast.14, bf16[512,2048]{1,0:T(8,128)(2,1)} %get-tuple-element.14.query_in), custom_call_target="tpu_custom_call" | custom-call | tf_op jit(solution)/shard_map/scatter_grads/pallas_call | solution.py:502
  173.0 3.2 %copy.29 = bf16[128,8192]{1,0:T(8,128)(2,1)} copy(bf16[128,8192]{1,0:T(8,128)(2,1)} %get-tuple-element.24) | data formatting | bytes 4194304
  176.1 0.7 copy.30
  176.8 0.7 copy.31
  (18 shorter events, 0.2 us)
Async XLA Ops:
  172.9 3.2 %copy-start.1 = (bf16[128,1024]{1,0:T(8,128)(2,1)S(1)}, bf16[128,1024]{1,0:T(8,128)(2,1)}, u32[]{:S(2)}) copy-start(bf16[128,1024]{1,0:T(8,128)(2,1)} %get-tuple-element.25) | copy-start | bytes 786436
  172.9 3.9 %copy-start = (bf16[128,1024]{1,0:T(8,128)(2,1)S(1)}, bf16[128,1024]{1,0:T(8,128)(2,1)}, u32[]{:S(2)}) copy-start(bf16[128,1024]{1,0:T(8,128)(2,1)} %get-tuple-element.26) | copy-start | bytes 786436
